TPU v7x, 512 devices: a whole 4x4x16 slice. The times are simulated.
512 devices in a mesh: major: 32 (over z_lo, y, core), minor: 16 (over z_hi, x).
Axes of the slice: x: 4, y: 4, z: 16 (z_hi: 4, z_lo: 4; z = z_hi * 4 + z_lo), core: 2. Of those that a mesh axis runs over, the one named last changes fastest.
Arguments:
- sequence_input: bfloat16 [4, 65536, 512], P(None, ('major', 'minor')), may hold values from -6 to 6
- first_depthwise_taps: float32 [3, 512], replicated, may hold values from -1 to 1
- first_norm_gain: float32 [512], replicated, may hold values from 0.5 to 1.5
- first_up_weight: bfloat16 [512, 1024], replicated, may hold values from -0.25 to 0.25
- first_down_weight: bfloat16 [1024, 512], replicated, may hold values from -0.1875 to 0.1875
- second_depthwise_taps: float32 [3, 512], replicated, may hold values from -1 to 1
- second_norm_gain: float32 [512], replicated, may hold values from 0.5 to 1.5
- second_up_weight: bfloat16 [512, 1024], replicated, may hold values from -0.25 to 0.25
- second_down_weight: bfloat16 [1024, 512], replicated, may hold values from -0.1875 to 0.1875
- pool_one: float32 [3, 512], replicated, may hold values from -1 to 1
- pool_two: float32 [3, 512], replicated, may hold values from -1 to 1
- pooled_cotangent: bfloat16 [4, 16384, 512], P(None, ('major', 'minor')), may hold values from -6 to 6
Outputs:
- pooled: bfloat16 [4, 16384, 512], P(None, ('major', 'minor'))
- input_grad: bfloat16 [4, 65536, 512], P(None, ('major', 'minor'))
All inputs are finite; a program needn't handle non-finite values.
Results may differ from a plain program's by a relative error of at most 0.013.
Values may be sent and summed in bfloat16 or wider, within the bound.
A program may use at most 64 MiB of HBM per device.

v0:
```python
from functools import partial

import jax
import jax.numpy as jnp
from jax import lax
from jax.sharding import PartitionSpec as P

BINS_PER_DEVICE = 128
FIRST_DILATION = 256
SECOND_DILATION = 1024


def shifted(block, axis, distance):
    devices = range(lax.axis_size(axis))
    route = [(i - distance, i) for i in devices if i - distance in devices]
    return lax.ppermute(block, axis, route)


def far_rows(value, count):
    return shifted(value, ("major", "minor"), count)


def matmul_rows(left, right):
    flat = left.reshape(-1, left.shape[-1])
    result = jnp.dot(flat, right, preferred_element_type=jnp.float32)
    return result.reshape(left.shape[:-1] + (right.shape[-1],))


def block_forward(x, lowered, raised, taps, gain, up, down):
    xf = x.astype(jnp.float32)
    conv = (
        taps[0] * lowered.astype(jnp.float32) + taps[1] * xf + taps[2] * raised.astype(jnp.float32)
    )
    scale = lax.rsqrt(jnp.mean(conv * conv, -1, keepdims=True) + 1e-06)
    normed = (conv * scale * gain).astype(jnp.bfloat16)
    hidden_pre = matmul_rows(normed, up)
    hidden = jax.nn.gelu(hidden_pre, approximate=True).astype(jnp.bfloat16)
    out = (xf + matmul_rows(hidden, down)).astype(jnp.bfloat16)
    return (out, conv, scale, hidden_pre)


def block_grad_conv(grad_out, conv, scale, hidden_pre, gain, up, down):
    grad_b = grad_out.astype(jnp.bfloat16)
    grad_hidden = matmul_rows(grad_b, down.T)
    pull = jax.vjp(partial(jax.nn.gelu, approximate=True), hidden_pre)[1]
    grad_pre = pull(grad_hidden)[0].astype(jnp.bfloat16)
    grad_norm = matmul_rows(grad_pre, up.T)
    scaled = grad_norm * gain
    return (
        scale * scaled - conv * (scale * scale * scale) * jnp.mean(scaled * conv, -1, keepdims=True)
    ).astype(jnp.bfloat16)


def pool_rows(prev, even, odd, taps):
    return taps[0] * prev + taps[1] * even + taps[2] * odd


def pool_step(value, rim, taps):
    batch, rows, width = value.shape
    pairs = value.astype(jnp.float32).reshape(batch, rows // 2, 2, width)
    even = pairs[:, :, 0]
    odd = pairs[:, :, 1]
    prev = jnp.concatenate([rim.astype(jnp.float32), odd[:, :-1]], 1)
    return pool_rows(prev, even, odd, taps).astype(jnp.bfloat16)


def unpool(grad, head, taps):
    batch, rows, width = grad.shape
    following = jnp.concatenate([grad[:, 1:], head], 1)
    even_part = taps[1] * grad
    odd_part = taps[2] * grad + taps[0] * following
    return jnp.stack([even_part, odd_part], 2).reshape(batch, 2 * rows, width)


def body(
    sequence_input,
    first_depthwise_taps,
    first_norm_gain,
    first_up_weight,
    first_down_weight,
    second_depthwise_taps,
    second_norm_gain,
    second_up_weight,
    second_down_weight,
    pool_one,
    pool_two,
    pooled_cotangent,
):
    block_list = (
        (
            first_depthwise_taps,
            first_norm_gain,
            first_up_weight,
            first_down_weight,
            FIRST_DILATION // BINS_PER_DEVICE,
        ),
        (
            second_depthwise_taps,
            second_norm_gain,
            second_up_weight,
            second_down_weight,
            SECOND_DILATION // BINS_PER_DEVICE,
        ),
    )
    current = sequence_input
    saved = []
    for taps, gain, up, down, span in block_list:
        lowered = far_rows(current, span)
        raised = far_rows(current, -span)
        current, conv, scale, hidden_pre = block_forward(
            current, lowered, raised, taps, gain, up, down
        )
        saved.append((conv, scale, hidden_pre))
    rows = current.shape[1]
    rim = shifted(current[:, rows - 1 :], ("major", "minor"), 1)
    middle = pool_step(current, rim, pool_one)
    mid_rows = middle.shape[1]
    rim_mid = shifted(middle[:, mid_rows - 1 :], ("major", "minor"), 1)
    pooled = pool_step(middle, rim_mid, pool_two)
    head = shifted(pooled_cotangent[:, :1], ("major", "minor"), -1).astype(jnp.float32)
    grad_mid = unpool(pooled_cotangent.astype(jnp.float32), head, pool_two)
    head_mid = shifted(grad_mid[:, :1], ("major", "minor"), -1)
    grad = unpool(grad_mid, head_mid, pool_one)
    for index in (1, 0):
        taps, gain, up, down, span = block_list[index]
        conv, scale, hidden_pre = saved[index]
        grad_conv = block_grad_conv(grad, conv, scale, hidden_pre, gain, up, down)
        lowered = far_rows(grad_conv, span)
        raised = far_rows(grad_conv, -span)
        grad = (
            grad
            + taps[0] * raised.astype(jnp.float32)
            + taps[1] * grad_conv.astype(jnp.float32)
            + taps[2] * lowered.astype(jnp.float32)
        )
    return (pooled, grad.astype(jnp.bfloat16))


def solution(mesh):
    placed = (
        P(None, ("major", "minor"), None),
        P(),
        P(),
        P(),
        P(),
        P(),
        P(),
        P(),
        P(),
        P(),
        P(),
        P(None, ("major", "minor"), None),
    )
    return jax.shard_map(
        body,
        mesh=mesh,
        in_specs=placed,
        out_specs=(P(None, ("major", "minor"), None), P(None, ("major", "minor"), None)),
        check_vma=False,
    )
```

profile of v0, /device:TPU:34, one launch (start us, length us, event | category | flops | bytes accessed | tf_op | source)
XLA Modules:
  0.0 366.3 jit_solution(9226564790178638375)
XLA Ops:
  0.7 1.6 copy.27
  2.2 4.0 %collective-permute-start = (bf16[4,128,512]{2,0,1:T(4,128)(2,1)S(1)}, bf16[4,128,512]{2,0,1:T(4,128)(2,1)S(1)}, u32[]{:S(2)}, u32[]{:S(2)}) collective-permute-start(bf16[4,128,512]{2,0,1:T(4,128)(2,1)S(1)} %copy.27), channel_id=1, source_target_pairs={{0,2},{1,3},{2,4},{3,5},{4,6},{5,7},{6,8},{7,9},{8,10},{9,11},{10,... | collective-permute-start | bytes 1572872 | tf_op jit(solution)/shard_map/ppermute | solution.py:16
  6.3 13.6 %collective-permute-start.1 = (bf16[4,128,512]{2,0,1:T(4,128)(2,1)S(1)}, bf16[4,128,512]{2,0,1:T(4,128)(2,1)S(1)}, u32[]{:S(2)}, u32[]{:S(2)}) collective-permute-start(bf16[4,128,512]{2,0,1:T(4,128)(2,1)S(1)} %copy.27), channel_id=1, source_target_pairs={{2,0},{3,1},{4,2},{5,3},{6,4},{7,5},{8,6},{9,7},{10,8},{11,9},{12,... | collective-permute-start | bytes 1572872 | tf_op jit(solution)/shard_map/ppermute | solution.py:16
  19.9 0.8 slice.120
  20.7 3.3 collective-permute-start.6
  24.0 1.0 copy_convert_fusion
  25.0 0.8 fusion.104
  25.8 0.8 fusion.103
  26.7 0.8 fusion.102
  27.5 0.8 fusion.101
  28.7 38.3 %collective-permute-start.7 = (f32[4,1,512]{2,0,1:T(4,128)S(1)}, f32[4,1,512]{2,0,1:T(4,128)S(1)}, u32[]{:S(2)}, u32[]{:S(2)}) collective-permute-start(f32[4,1,512]{2,0,1:T(4,128)S(1)} %slice.122), channel_id=1, source_target_pairs={{1,0},{2,1},{3,2},{4,3},{5,4},{6,5},{7,6},{8,7},{9,8},{10,9},{11,1... | collective-permute-start | bytes 24584 | tf_op jit(solution)/shard_map/ppermute | solution.py:16
  67.2 0.9 multiply_reduce_fusion.3
  68.2 0.9 multiply_convert_fusion.5
  69.1 0.7 fusion.38
  70.3 0.8 fusion.35
  71.6 0.9 fusion.20
  72.6 6.7 %collective-permute-start.3 = (bf16[4,128,512]{2,0,1:T(4,128)(2,1)S(1)}, bf16[4,128,512]{2,0,1:T(4,128)(2,1)S(1)}, u32[]{:S(2)}, u32[]{:S(2)}) collective-permute-start(bf16[4,128,512]{2,0,1:T(4,128)(2,1)S(1)} %fusion.20), channel_id=1, source_target_pairs={{8,0},{9,1},{10,2},{11,3},{12,4},{13,5},{14,6},{15,7},{16,8},{17,9... | collective-permute-start | bytes 1572872 | tf_op jit(solution)/shard_map/ppermute | solution.py:16
  79.3 8.1 %collective-permute-start.2 = (bf16[4,128,512]{2,0,1:T(4,128)(2,1)S(1)}, bf16[4,128,512]{2,0,1:T(4,128)(2,1)S(1)}, u32[]{:S(2)}, u32[]{:S(2)}) collective-permute-start(bf16[4,128,512]{2,0,1:T(4,128)(2,1)S(1)} %fusion.20), channel_id=1, source_target_pairs={{0,8},{1,9},{2,10},{3,11},{4,12},{5,13},{6,14},{7,15},{8,16},{9,17... | collective-permute-start | bytes 1572872 | tf_op jit(solution)/shard_map/ppermute | solution.py:16
  88.0 1.0 bitcast_convert_fusion
  89.0 106.5 %collective-permute-done.3 = bf16[4,128,512]{2,0,1:T(4,128)(2,1)S(1)} collective-permute-done((bf16[4,128,512]{2,0,1:T(4,128)(2,1)S(1)}, bf16[4,128,512]{2,0,1:T(4,128)(2,1)S(1)}, u32[]{:S(2)}, u32[]{:S(2)}) %collective-permute-start.3) | collective-permute-done | bytes 524320 | tf_op jit(solution)/shard_map/ppermute | solution.py:16
  195.5 38.7 %collective-permute-done.2 = bf16[4,128,512]{2,0,1:T(4,128)(2,1)S(1)} collective-permute-done((bf16[4,128,512]{2,0,1:T(4,128)(2,1)S(1)}, bf16[4,128,512]{2,0,1:T(4,128)(2,1)S(1)}, u32[]{:S(2)}, u32[]{:S(2)}) %collective-permute-start.2) | collective-permute-done | bytes 524320 | tf_op jit(solution)/shard_map/ppermute | solution.py:16
  234.2 0.8 multiply_reduce_fusion.2
  235.0 0.8 multiply_convert_fusion.2
  235.8 0.7 fusion.31
  236.6 1.3 copy-done.15
  237.9 1.8 fusion.28
  239.7 5.2 %fusion.14 = f32[4,128,512]{2,1,0:T(8,128)} fusion(f32[4,128,1024]{2,1,0:T(8,128)} %copy-done.15, bf16[1024,512]{1,0:T(8,128)(2,1)} %param.20, bf16[512,1024]{1,0:T(8,128)(2,1)S(1)} %copy-done, bf16[4,128,512]{2,0,1:T(4,128)(2,1)} %bitcast_convert_fusion), kind=kOutput, calls=%fused_computation.20 | convolution fusion | flops 1084227584 | bytes 5767168 | tf_op jit(solution)/shard_map/dot_general | solution.py:25
  244.9 2.8 multiply_reduce_fusion.1
  247.7 3.2 subtract_convert_fusion.1
  250.9 1.9 collective-permute-start.9
  252.8 13.6 %collective-permute-start.8 = (bf16[4,128,512]{2,0,1:T(4,128)(2,1)S(1)}, bf16[4,128,512]{2,0,1:T(4,128)(2,1)S(1)}, u32[]{:S(2)}, u32[]{:S(2)}) collective-permute-start(bf16[4,128,512]{2,0,1:T(4,128)(2,1)S(1)} %get-tuple-element.8), channel_id=1, source_target_pairs={{8,0},{9,1},{10,2},{11,3},{12,4},{13,5},{14,6},{15,7},{16,8},{17,9... | collective-permute-start | bytes 1572872 | tf_op jit(solution)/shard_map/ppermute | solution.py:16
  266.4 1.9 collective-permute-start.4
  268.7 1.2 fusion.100
  270.0 24.6 %collective-permute-done.4 = bf16[4,1,512]{2,0,1:T(4,128)(2,1)S(1)} collective-permute-done((bf16[4,1,512]{2,0,1:T(4,128)(2,1)S(1)}, bf16[4,1,512]{2,0,1:T(4,128)(2,1)S(1)}, u32[]{:S(2)}, u32[]{:S(2)}) %collective-permute-start.4) | collective-permute-done | bytes 4128 | tf_op jit(solution)/shard_map/ppermute | solution.py:16
  294.5 2.1 collective-permute-start.5
  296.7 0.9 pad_maximum_fusion.1
  297.6 0.8 copy-done.19
  298.4 0.8 copy-done.21
  299.2 1.6 fusion.99
  300.8 5.4 %fusion.15 = f32[4,128,512]{2,1,0:T(8,128)} fusion(f32[4,128,1024]{2,1,0:T(8,128)} %copy-done.14, bf16[1024,512]{1,0:T(8,128)(2,1)} %param.16, bf16[512,1024]{1,0:T(8,128)(2,1)} %param.15, bf16[4,128,512]{2,0,1:T(4,128)(2,1)} %fusion.99), kind=kOutput, calls=%fused_computation.21 | convolution fusion | flops 1084227584 | bytes 5767168 | tf_op jit(solution)/shard_map/dot_general | solution.py:25
  306.3 2.7 multiply_reduce_fusion
  309.1 1.7 subtract_convert_fusion
  310.8 1.9 collective-permute-start.11
  312.7 22.1 %collective-permute-start.10 = (bf16[4,128,512]{2,0,1:T(4,128)(2,1)S(1)}, bf16[4,128,512]{2,0,1:T(4,128)(2,1)S(1)}, u32[]{:S(2)}, u32[]{:S(2)}) collective-permute-start(bf16[4,128,512]{2,0,1:T(4,128)(2,1)S(1)} %subtract_convert_fusion), channel_id=1, source_target_pairs={{2,0},{3,1},{4,2},{5,3},{6,4},{7,5},{8,6},{9,7},{10,8},{11,9},{12,... | collective-permute-start | bytes 1572872 | tf_op jit(solution)/shard_map/ppermute | solution.py:16
  335.4 0.7 copy.46
  336.0 27.9 %collective-permute-done.11 = bf16[4,128,512]{2,0,1:T(4,128)(2,1)S(1)} collective-permute-done((bf16[4,128,512]{2,0,1:T(4,128)(2,1)S(1)}, bf16[4,128,512]{2,0,1:T(4,128)(2,1)S(1)}, u32[]{:S(2)}, u32[]{:S(2)}) %collective-permute-start.11) | collective-permute-done | bytes 524320 | tf_op jit(solution)/shard_map/ppermute | solution.py:16
  364.0 1.4 add_convert_fusion
  365.4 0.9 copy.47
  (89 shorter events, 3.2 us)
Async XLA Ops:
  0.6 235.2 %copy-start = (bf16[512,1024]{1,0:T(8,128)(2,1)S(1)}, bf16[512,1024]{1,0:T(8,128)(2,1)}, u32[]{:S(2)}) copy-start(bf16[512,1024]{1,0:T(8,128)(2,1)} %param.19) | copy-start | bytes 3145732
  0.6 27.7 %copy-start.24 = (bf16[4,32,512]{2,1,0:T(8,128)(2,1)S(1)}, bf16[4,32,512]{2,1,0:T(8,128)(2,1)}, u32[]{:S(2)}) copy-start(bf16[4,32,512]{2,1,0:T(8,128)(2,1)} %param.23) | copy-start | bytes 393220
  2.2 64.9 %collective-permute-start = (bf16[4,128,512]{2,0,1:T(4,128)(2,1)S(1)}, bf16[4,128,512]{2,0,1:T(4,128)(2,1)S(1)}, u32[]{:S(2)}, u32[]{:S(2)}) collective-permute-start(bf16[4,128,512]{2,0,1:T(4,128)(2,1)S(1)} %copy.27), channel_id=1, source_target_pairs={{0,2},{1,3},{2,4},{3,5},{4,6},{5,7},{6,8},{7,9},{8,10},{9,11},{10,... | collective-permute-start | bytes 1572872 | tf_op jit(solution)/shard_map/ppermute | solution.py:16
  6.3 60.9 %collective-permute-start.1 = (bf16[4,128,512]{2,0,1:T(4,128)(2,1)S(1)}, bf16[4,128,512]{2,0,1:T(4,128)(2,1)S(1)}, u32[]{:S(2)}, u32[]{:S(2)}) collective-permute-start(bf16[4,128,512]{2,0,1:T(4,128)(2,1)S(1)} %copy.27), channel_id=1, source_target_pairs={{2,0},{3,1},{4,2},{5,3},{6,4},{7,5},{8,6},{9,7},{10,8},{11,9},{12,... | collective-permute-start | bytes 1572872 | tf_op jit(solution)/shard_map/ppermute | solution.py:16
  20.7 7.7 %collective-permute-start.6 = (bf16[4,1,512]{2,0,1:T(4,128)(2,1)S(1)}, bf16[4,1,512]{2,0,1:T(4,128)(2,1)S(1)}, u32[]{:S(2)}, u32[]{:S(2)}) collective-permute-start(bf16[4,1,512]{2,0,1:T(4,128)(2,1)S(1)} %copy.86), channel_id=1, source_target_pairs={{1,0},{2,1},{3,2},{4,3},{5,4},{6,5},{7,6},{8,7},{9,8},{10,9},{11,1... | collective-permute-start | bytes 12296 | tf_op jit(solution)/shard_map/ppermute | solution.py:16
  28.3 38.9 %copy-start.1 = (bf16[4,128,512]{2,1,0:T(8,128)(2,1)S(1)}, bf16[4,128,512]{2,1,0:T(8,128)(2,1)}, u32[]{:S(2)}) copy-start(bf16[4,128,512]{2,1,0:T(8,128)(2,1)} %param.12) | copy-start | bytes 1572868
  28.7 39.5 %copy-start.26 = (f32[512]{0:T(512)S(1)}, f32[512]{0:T(512)}, u32[]{:S(2)}) copy-start(f32[512]{0:T(512)} %param.14) | copy-start | bytes 6148
  28.7 58.6 %collective-permute-start.7 = (f32[4,1,512]{2,0,1:T(4,128)S(1)}, f32[4,1,512]{2,0,1:T(4,128)S(1)}, u32[]{:S(2)}, u32[]{:S(2)}) collective-permute-start(f32[4,1,512]{2,0,1:T(4,128)S(1)} %slice.122), channel_id=1, source_target_pairs={{1,0},{2,1},{3,2},{4,3},{5,4},{6,5},{7,6},{8,7},{9,8},{10,9},{11,1... | collective-permute-start | bytes 24584 | tf_op jit(solution)/shard_map/ppermute | solution.py:16
  67.1 1.9 copy-start.23
  67.2 2.6 copy-start.2
  67.2 2.6 copy-start.4
  69.0 1.2 copy-start.28
  70.3 1.4 copy-start.14
  72.6 122.9 %collective-permute-start.3 = (bf16[4,128,512]{2,0,1:T(4,128)(2,1)S(1)}, bf16[4,128,512]{2,0,1:T(4,128)(2,1)S(1)}, u32[]{:S(2)}, u32[]{:S(2)}) collective-permute-start(bf16[4,128,512]{2,0,1:T(4,128)(2,1)S(1)} %fusion.20), channel_id=1, source_target_pairs={{8,0},{9,1},{10,2},{11,3},{12,4},{13,5},{14,6},{15,7},{16,8},{17,9... | collective-permute-start | bytes 1572872 | tf_op jit(solution)/shard_map/ppermute | solution.py:16
  79.3 154.9 %collective-permute-start.2 = (bf16[4,128,512]{2,0,1:T(4,128)(2,1)S(1)}, bf16[4,128,512]{2,0,1:T(4,128)(2,1)S(1)}, u32[]{:S(2)}, u32[]{:S(2)}) collective-permute-start(bf16[4,128,512]{2,0,1:T(4,128)(2,1)S(1)} %fusion.20), channel_id=1, source_target_pairs={{0,8},{1,9},{2,10},{3,11},{4,12},{5,13},{6,14},{7,15},{8,16},{9,17... | collective-permute-start | bytes 1572872 | tf_op jit(solution)/shard_map/ppermute | solution.py:16
  88.0 147.0 %copy-start.25 = (f32[512]{0:T(512)S(1)}, f32[512]{0:T(512)}, u32[]{:S(2)}) copy-start(f32[512]{0:T(512)} %param.18) | copy-start | bytes 6148
  195.5 41.0 %copy-start.6 = (bf16[4,128,512]{2,0,1:T(4,128)(2,1)}, bf16[4,128,512]{2,0,1:T(4,128)(2,1)S(1)}, u32[]{:S(2)}) copy-start(bf16[4,128,512]{2,0,1:T(4,128)(2,1)S(1)} %collective-permute-done.3) | copy-start | bytes 1572868
  234.2 2.4 copy-start.8
  235.8 2.1 copy-start.27
  236.6 1.3 copy-start.15
  244.9 2.8 copy-start.7
  244.9 2.8 copy-start.9
  244.9 2.8 copy-start.12
  250.9 46.7 %copy-start.10 = (bf16[4,128,512]{2,0,1:T(4,128)(2,1)}, bf16[4,128,512]{2,0,1:T(4,128)(2,1)S(1)}, u32[]{:S(2)}) copy-start(bf16[4,128,512]{2,0,1:T(4,128)(2,1)S(1)} %get-tuple-element.8) | copy-start | bytes 1572868
  250.9 46.7 %collective-permute-start.9 = (bf16[4,128,512]{2,0,1:T(4,128)(2,1)S(1)}, bf16[4,128,512]{2,0,1:T(4,128)(2,1)S(1)}, u32[]{:S(2)}, u32[]{:S(2)}) collective-permute-start(bf16[4,128,512]{2,0,1:T(4,128)(2,1)S(1)} %get-tuple-element.8), channel_id=1, source_target_pairs={{0,8},{1,9},{2,10},{3,11},{4,12},{5,13},{6,14},{7,15},{8,16},{9,17... | collective-permute-start | bytes 1572872 | tf_op jit(solution)/shard_map/ppermute | solution.py:16
  252.8 44.8 %collective-permute-start.8 = (bf16[4,128,512]{2,0,1:T(4,128)(2,1)S(1)}, bf16[4,128,512]{2,0,1:T(4,128)(2,1)S(1)}, u32[]{:S(2)}, u32[]{:S(2)}) collective-permute-start(bf16[4,128,512]{2,0,1:T(4,128)(2,1)S(1)} %get-tuple-element.8), channel_id=1, source_target_pairs={{8,0},{9,1},{10,2},{11,3},{12,4},{13,5},{14,6},{15,7},{16,8},{17,9... | collective-permute-start | bytes 1572872 | tf_op jit(solution)/shard_map/ppermute | solution.py:16
  266.4 28.1 %collective-permute-start.4 = (bf16[4,1,512]{2,0,1:T(4,128)(2,1)S(1)}, bf16[4,1,512]{2,0,1:T(4,128)(2,1)S(1)}, u32[]{:S(2)}, u32[]{:S(2)}) collective-permute-start(bf16[4,1,512]{2,0,1:T(4,128)(2,1)S(1)} %slice.108), channel_id=1, source_target_pairs={{0,1},{1,2},{2,3},{3,4},{4,5},{5,6},{6,7},{7,8},{8,9},{9,10},{10,1... | collective-permute-start | bytes 12296 | tf_op jit(solution)/shard_map/ppermute | solution.py:16
  294.5 40.7 %collective-permute-start.5 = (bf16[4,1,512]{2,0,1:T(4,128)(2,1)S(1)}, bf16[4,1,512]{2,0,1:T(4,128)(2,1)S(1)}, u32[]{:S(2)}, u32[]{:S(2)}) collective-permute-start(bf16[4,1,512]{2,0,1:T(4,128)(2,1)S(1)} %fusion.77), channel_id=1, source_target_pairs={{0,1},{1,2},{2,3},{3,4},{4,5},{5,6},{6,7},{7,8},{8,9},{9,10},{10,1... | collective-permute-start | bytes 12296 | tf_op jit(solution)/shard_map/ppermute | solution.py:16
  297.6 0.8 copy-start.19
  298.4 0.8 copy-start.21
  300.8 5.4 %copy-start.3 = (bf16[4,128,512]{2,0,1:T(4,128)(2,1)S(1)}, bf16[4,128,512]{2,0,1:T(4,128)(2,1)}, u32[]{:S(2)}) copy-start(bf16[4,128,512]{2,0,1:T(4,128)(2,1)} %copy-done.2) | copy-start | bytes 1572868
  306.3 2.8 copy-start.5
  306.3 2.8 copy-start.13
  309.0 25.7 %copy-start.16 = (f32[4,64,512]{2,0,1:T(4,128)S(1)}, f32[4,64,512]{2,0,1:T(4,128)}, u32[]{:S(2)}) copy-start(f32[4,64,512]{2,0,1:T(4,128)} %pad_maximum_fusion.1) | copy-start | bytes 1572868
  309.0 25.8 %copy-start.17 = (f32[4,64,1,512]{3,0,2,1:T(4,128)S(1)}, f32[4,64,1,512]{3,0,2,1:T(4,128)}, u32[]{:S(2)}) copy-start(f32[4,64,1,512]{3,0,2,1:T(4,128)} %get-tuple-element.12) | copy-start | bytes 1572868
  309.0 25.8 %copy-start.18 = (f32[4,64,1,512]{3,0,2,1:T(4,128)S(1)}, f32[4,64,1,512]{3,0,2,1:T(4,128)}, u32[]{:S(2)}) copy-start(f32[4,64,1,512]{3,0,2,1:T(4,128)} %get-tuple-element.13) | copy-start | bytes 1572868
  310.8 53.2 %collective-permute-start.11 = (bf16[4,128,512]{2,0,1:T(4,128)(2,1)S(1)}, bf16[4,128,512]{2,0,1:T(4,128)(2,1)S(1)}, u32[]{:S(2)}, u32[]{:S(2)}) collective-permute-start(bf16[4,128,512]{2,0,1:T(4,128)(2,1)S(1)} %subtract_convert_fusion), channel_id=1, source_target_pairs={{0,2},{1,3},{2,4},{3,5},{4,6},{5,7},{6,8},{7,9},{8,10},{9,11},{10,... | collective-permute-start | bytes 1572872 | tf_op jit(solution)/shard_map/ppermute | solution.py:16
  312.7 51.3 %collective-permute-start.10 = (bf16[4,128,512]{2,0,1:T(4,128)(2,1)S(1)}, bf16[4,128,512]{2,0,1:T(4,128)(2,1)S(1)}, u32[]{:S(2)}, u32[]{:S(2)}) collective-permute-start(bf16[4,128,512]{2,0,1:T(4,128)(2,1)S(1)} %subtract_convert_fusion), channel_id=1, source_target_pairs={{2,0},{3,1},{4,2},{5,3},{6,4},{7,5},{8,6},{9,7},{10,8},{11,9},{12,... | collective-permute-start | bytes 1572872 | tf_op jit(solution)/shard_map/ppermute | solution.py:16
  334.8 29.2 %copy-start.11 = (bf16[4,128,512]{2,0,1:T(4,128)(2,1)S(1)}, bf16[4,128,512]{2,0,1:T(4,128)(2,1)}, u32[]{:S(2)}) copy-start(bf16[4,128,512]{2,0,1:T(4,128)(2,1)} %copy-done.10) | copy-start | bytes 1572868
  334.8 29.2 %copy-start.20 = (bf16[4,128,512]{2,0,1:T(4,128)(2,1)S(1)}, bf16[4,128,512]{2,0,1:T(4,128)(2,1)}, u32[]{:S(2)}) copy-start(bf16[4,128,512]{2,0,1:T(4,128)(2,1)} %copy-done.19) | copy-start | bytes 1572868
  334.8 29.2 %copy-start.22 = (bf16[4,128,512]{2,0,1:T(4,128)(2,1)S(1)}, bf16[4,128,512]{2,0,1:T(4,128)(2,1)}, u32[]{:S(2)}) copy-start(bf16[4,128,512]{2,0,1:T(4,128)(2,1)} %copy-done.21) | copy-start | bytes 1572868
where the time goes:
time: 367 us; the launch traced here: 366 us
  waiting for transfers between devices  198 us (54%)
  starting transfers between devices  118 us (32%)
  other arithmetic  22.3 us (6%)
  matrix products  14.7 us (4%)
  local copies, waits for them, and re-layouts  12.8 us (3%)
    ppermute x12, waiting for transfers between devices, shifted(): return lax.ppermute(block, axis, route)  198 us
    ppermute x12, starting transfers between devices, shifted(): return lax.ppermute(block, axis, route)  118 us
    dot_general x6, matrix products, matmul_rows(): result = jnp.dot(flat, right, preferred_element_type=jnp.float32)  14.7 us
  transfers between devices with their start and end apart: 12, of which 4 were waited for; matrix products, arithmetic and copies ran while one was open for 7% of the time, Pallas kernels for 0%

commit v1 on v0

v1 whole, which is shorter than its diff:
```python
import jax
import jax.numpy as jnp
from jax import lax
from jax.experimental import pallas as pl
from jax.experimental.pallas import tpu as pltpu
from jax.sharding import PartitionSpec as P

MESH = pl.DeviceIdType.MESH
F32 = jnp.float32
BF16 = jnp.bfloat16

C = 512
HID = 1024
MAJOR = 32
POS = 8
SUB = 4
ROWS = 16
CHUNK = SUB * ROWS
M = POS * ROWS
GELU_A = 0.7978845608028654
GELU_B = 0.044715


def dot(left, right):
    return jnp.dot(left, right, preferred_element_type=F32)


def one_hot(shape, match):
    row = lax.broadcasted_iota(jnp.int32, shape, 0)
    col = lax.broadcasted_iota(jnp.int32, shape, 1)
    return match(row, col).astype(F32).astype(BF16)


def rows_of(value):
    return value.reshape(-1, C)


def gelu_parts(a):
    square = a * a
    t = jnp.tanh(GELU_A * a * (1.0 + GELU_B * square))
    half = 0.5 + 0.5 * t
    slope = half + 0.5 * a * (1.0 - t * t) * (GELU_A * (1.0 + 3.0 * GELU_B * square))
    return a * half, slope


def kernel(
    x_ref, taps1, gain1, up1_hbm, down1_hbm, taps2, gain2, up2_hbm, down2_hbm, pool1, pool2, g_ref,
    pooled_ref, out_ref,
    xbuf, x1buf, gc2buf, gc1buf, gbuf, grimbuf, grim_a, grim_b, rimbuf, rim_a, rim_b,
    conv1, scale1, slope1, gy2, gy1, x2buf, obuf, pbuf, xsel, midb,
    up1, down1, up2, down2, up1t, down1t, up2t, down2t,
    xs, xr, gs, gr, hs, hr, os, orr, ps, pr, rs, rr, ws, loc,
):
    major, minor = lax.axis_index("major"), lax.axis_index("minor")
    zhi, x = minor // 4, minor % 4
    half, low = x // 2, x % 2
    me = zhi * 2 + half
    first, last = major == 0, major == MAJOR - 1
    head, tail = x == 0, x == 3

    def member(j):
        return (major, (j // 2) * 4 + (j % 2) * 2 + low)

    below, above = (major - 1, minor), (major + 1, minor)
    next_x = jnp.where(half == 0, x + 2, 1 - low)
    prev_x = jnp.where(half == 1, x - 2, 3 - low)
    follow, before = (major, zhi * 4 + next_x), (major, zhi * 4 + prev_x)
    over, under = (major + 1, zhi * 4), (major - 1, zhi * 4 + 3)
    side = (major, zhi * 4 + 3 - x)

    barrier = pltpu.get_barrier_semaphore()

    def greet(device):
        pl.semaphore_signal(barrier, inc=1, device_id=device, device_id_type=MESH)

    for step in range(1, POS):
        greet(member((me + step) % POS))
    greet(side)
    pl.when(jnp.logical_not(first))(lambda: greet(below))
    pl.when(jnp.logical_not(last))(lambda: greet(above))
    pl.when(jnp.logical_and(tail, jnp.logical_not(last)))(lambda: greet(over))
    pl.when(jnp.logical_and(head, jnp.logical_not(first)))(lambda: greet(under))

    weight_copies = [
        pltpu.make_async_copy(source, target, ws.at[k])
        for k, (source, target) in enumerate(
            ((up1_hbm, up1), (down1_hbm, down1), (up2_hbm, up2), (down2_hbm, down2))
        )
    ]
    for copy in weight_copies:
        copy.start()

    def remote(source, target, send, recv, device):
        return pltpu.make_async_remote_copy(
            src_ref=source, dst_ref=target, send_sem=send, recv_sem=recv,
            device_id=device, device_id_type=MESH,
        )

    def x_rows(j, s):
        return x_ref.at[j // 2, pl.ds((j % 2) * CHUNK + s * ROWS, ROWS)]

    def x_send(j, s):
        return remote(x_rows(j, s), xbuf.at[s, 1 + me], xs.at[s, j], xr.at[s, me], member(j))

    def x_recv(j, s):
        return remote(x_rows(j, s), xbuf.at[s, 1 + j], xs.at[s, j], xr.at[s, j], member(j))

    def x_local(s):
        return pltpu.make_async_copy(x_rows(me, s), xbuf.at[s, 1 + me], xr.at[s, me])

    def g_rows(j):
        return g_ref.at[j // 2, pl.ds((j % 2) * 16, 16)]

    def g_send(j):
        return remote(g_rows(j), gbuf.at[me], gs.at[j], gr.at[me], member(j))

    def g_recv(j):
        return remote(g_rows(j), gbuf.at[j], gs.at[j], gr.at[j], member(j))

    def g_local():
        return pltpu.make_async_copy(g_rows(me), gbuf.at[me], gr.at[me])

    def out_rows(s):
        return out_ref.at[zhi, pl.ds(half * CHUNK + s * ROWS, ROWS)]

    def o_send(j, s):
        return remote(obuf.at[s, j], out_rows(s), os.at[s, j], orr.at[s, me], member(j))

    def o_recv(j, s):
        rows = out_ref.at[j // 2, pl.ds((j % 2) * CHUNK + s * ROWS, ROWS)]
        return remote(obuf.at[s, j], rows, os.at[s, j], orr.at[s, j], member(j))

    def o_local(s):
        return pltpu.make_async_copy(obuf.at[s, me], out_rows(s), orr.at[s, me])

    def p_send(j):
        rows = pooled_ref.at[zhi, pl.ds(half * 16, 16)]
        return remote(pbuf.at[j], rows, ps.at[j], pr.at[me], member(j))

    def p_recv(j):
        rows = pooled_ref.at[j // 2, pl.ds((j % 2) * 16, 16)]
        return remote(pbuf.at[j], rows, ps.at[j], pr.at[j], member(j))

    def p_local():
        return pltpu.make_async_copy(pbuf.at[me], pooled_ref.at[zhi, pl.ds(half * 16, 16)], pr.at[me])

    def halo_down(kind, buf, reach, s):
        return remote(
            buf.at[s, pl.ds(reach, reach)], buf.at[s, pl.ds(reach + POS, reach)],
            hs.at[kind, s, 0], hr.at[kind, s, 0], below,
        )

    def halo_up(kind, buf, reach, s):
        return remote(
            buf.at[s, pl.ds(POS, reach)], buf.at[s, pl.ds(0, reach)],
            hs.at[kind, s, 1], hr.at[kind, s, 1], above,
        )

    def send_halos(kind, buf, reach, s):
        pl.when(jnp.logical_not(first))(lambda: halo_down(kind, buf, reach, s).start())
        pl.when(jnp.logical_not(last))(lambda: halo_up(kind, buf, reach, s).start())

    def wait_halos(kind, buf, reach, s):
        pl.when(jnp.logical_not(last))(lambda: halo_down(kind, buf, reach, s).wait_recv())
        pl.when(jnp.logical_not(first))(lambda: halo_up(kind, buf, reach, s).wait_recv())

    halos = ((xbuf, 1), (x1buf, 4), (gc2buf, 4), (gc1buf, 1))

    for buf, reach in halos:
        zeros = jnp.zeros((SUB, reach, ROWS, C), BF16)

        @pl.when(first)
        def _(buf=buf, reach=reach, zeros=zeros):
            buf[:, pl.ds(0, reach)] = zeros

        @pl.when(last)
        def _(buf=buf, reach=reach, zeros=zeros):
            buf[:, pl.ds(reach + POS, reach)] = zeros

    has_under = jnp.logical_and(head, jnp.logical_not(first))
    has_over = jnp.logical_and(tail, jnp.logical_not(last))

    @pl.when(jnp.logical_not(has_under))
    def _():
        rim_b[...] = jnp.zeros((16, C), BF16)

    @pl.when(jnp.logical_not(has_over))
    def _():
        grim_b[...] = jnp.zeros((16, C), BF16)

    partners = (
        POS
        + jnp.where(first, 0, 1) + jnp.where(last, 0, 1)
        + jnp.where(has_over, 1, 0) + jnp.where(has_under, 1, 0)
    )
    pl.semaphore_wait(barrier, partners)

    def send_x(s):
        for step in range(1, POS):
            x_send((me + step) % POS, s).start()
        x_local(s).start()

    send_x(0)
    send_x(1)
    for step in range(1, POS):
        g_send((me + step) % POS).start()
    g_local().start()
    send_x(2)
    send_x(3)

    for copy in weight_copies:
        copy.wait()
    up1t[...] = up1[...].T
    down1t[...] = down1[...].T
    up2t[...] = up2[...].T
    down2t[...] = down2[...].T

    def forward(buf, reach, s, taps, gain, up, down):
        lowered = rows_of(buf[s, pl.ds(0, POS)]).astype(F32)
        here = rows_of(buf[s, pl.ds(reach, POS)]).astype(F32)
        raised = rows_of(buf[s, pl.ds(2 * reach, POS)]).astype(F32)
        conv = taps[0:1] * lowered + taps[1:2] * here + taps[2:3] * raised
        scale = lax.rsqrt(jnp.mean(conv * conv, -1, keepdims=True) + 1e-06)
        normed = (conv * scale * gain[...]).astype(BF16)
        hidden, slope = gelu_parts(dot(normed, up[...]))
        out = (here + dot(hidden.astype(BF16), down[...])).astype(BF16)
        return out, conv, scale, slope

    def backward(grad, conv, scale, slope, gain, upt, downt):
        grad_pre = (slope * dot(grad.astype(BF16), downt[...])).astype(BF16)
        scaled = dot(grad_pre, upt[...]) * gain[...]
        mean = jnp.mean(scaled * conv, -1, keepdims=True)
        return (scale * scaled - conv * (scale * scale * scale) * mean).astype(BF16)

    def spread(grad, buf, reach, s, taps):
        lowered = rows_of(buf[s, pl.ds(0, POS)]).astype(F32)
        here = rows_of(buf[s, pl.ds(reach, POS)]).astype(F32)
        raised = rows_of(buf[s, pl.ds(2 * reach, POS)]).astype(F32)
        return grad + taps[0:1] * raised + taps[1:2] * here + taps[2:3] * lowered

    def top_coefficients():
        one, two = [pool1[k : k + 1] for k in range(3)], [pool2[k : k + 1] for k in range(3)]
        here = (one[1] * two[1], one[2] * two[1] + one[0] * two[2], one[1] * two[2], one[2] * two[2])
        ahead = (jnp.zeros((1, C), F32), one[0] * two[0], one[1] * two[0], one[2] * two[0] + one[0] * two[1])
        place = lax.broadcasted_iota(jnp.int32, (M, C), 0) % 4

        def pick(four):
            return jnp.where(place == 0, four[0], jnp.where(place == 1, four[1], jnp.where(place == 2, four[2], four[3])))

        return pick(here), pick(ahead)

    def stage_a(s):
        for step in range(1, POS):
            x_recv((me + step) % POS, s).wait_recv()
        x_local(s).wait()
        send_halos(0, xbuf, 1, s)

    def stage_b(s):
        wait_halos(0, xbuf, 1, s)
        out, conv, scale, slope = forward(xbuf, 1, s, taps1, gain1, up1, down1)
        x1buf[s, pl.ds(4, POS)] = out.reshape(POS, ROWS, C)
        send_halos(1, x1buf, 4, s)
        conv1[s] = conv
        scale1[s] = scale
        slope1[s] = slope

    def take_g():
        for step in range(1, POS):
            g_recv((me + step) % POS).wait_recv()
        g_local().wait()
        firsts = one_hot((16, M), lambda row, col: jnp.logical_and(col == row * 16, row < POS))
        grimbuf[...] = dot(firsts, rows_of(gbuf[...])).astype(BF16)
        remote(grimbuf, grim_a, rs.at[0], rr.at[0], before).start()
        pl.when(has_under)(lambda: remote(grimbuf, grim_b, rs.at[1], rr.at[1], under).start())

    def stage_c(s):
        pl.when(s == 0)(take_g)
        coef_here, coef_ahead = top_coefficients()
        g_all = rows_of(gbuf[...])

        def take(row, col, ahead):
            return jnp.logical_and(row // ROWS == col // 16, (row % ROWS) // 4 + ahead + 4 * s == col % 16)

        here = dot(one_hot((M, M), lambda row, col: take(row, col, 0)), g_all)
        ahead = dot(one_hot((M, M), lambda row, col: take(row, col, 1)), g_all)
        gy2[s] = coef_here * here + coef_ahead * ahead

        @pl.when(s == SUB - 1)
        def _():
            remote(grimbuf, grim_a, rs.at[0], rr.at[0], before).wait_recv()
            pl.when(has_over)(lambda: remote(grimbuf, grim_b, rs.at[1], rr.at[1], over).wait_recv())
            shift = jnp.where(tail, 1, 0)

            def from_a(row, col):
                return jnp.logical_and(row % ROWS >= ROWS - 4, jnp.logical_and(row // ROWS + shift == col, col < POS))

            def from_b(row, col):
                return jnp.logical_and(row >= M - 4, col == 0)

            rim = dot(one_hot((M, 16), from_a), grim_a[...]) + dot(one_hot((M, 16), from_b), grim_b[...])
            gy2[s] = gy2[s] + coef_ahead * rim

        wait_halos(1, x1buf, 4, s)
        out, conv, scale, slope = forward(x1buf, 4, s, taps2, gain2, up2, down2)
        x2buf[s] = out
        grad_conv = backward(gy2[s], conv, scale, slope, gain2, up2t, down2t)
        gc2buf[s, pl.ds(4, POS)] = grad_conv.reshape(POS, ROWS, C)
        send_halos(2, gc2buf, 4, s)

    def stage_d(s):
        wait_halos(2, gc2buf, 4, s)
        grad = spread(gy2[s], gc2buf, 4, s, taps2)
        grad_conv = backward(grad, conv1[s], scale1[s], slope1[s], gain1, up1t, down1t)
        gc1buf[s, pl.ds(1, POS)] = grad_conv.reshape(POS, ROWS, C)
        send_halos(3, gc1buf, 1, s)
        gy1[s] = grad

    def stage_e(s):
        wait_halos(3, gc1buf, 1, s)
        obuf[s] = spread(gy1[s], gc1buf, 1, s, taps1).astype(BF16).reshape(POS, ROWS, C)
        for step in range(1, POS):
            o_send((me + step) % POS, s).start()
        o_local(s).start()

    def pool_first():
        def pick(r):
            def match(row, col):
                j, place, bin_ = row % 16, col % M, col % ROWS
                return jnp.logical_and(
                    jnp.logical_and(row // 16 == place // ROWS, j // 4 == col // M), 4 * (j % 4) + r == bin_
                )

            return one_hot((M, SUB * M), match)

        x2_all = x2buf[...].reshape(SUB * M, C)
        for r in range(4):
            xsel[r] = dot(pick(r), x2_all)
        midb[...] = (pool1[0:1] * xsel[1] + pool1[1:2] * xsel[2] + pool1[2:3] * xsel[3]).astype(BF16)
        last_x = one_hot((16, M), lambda row, col: jnp.logical_and(col == row * 16 + 15, row < POS))
        last_m = one_hot((16, M), lambda row, col: col == (row - POS) * 16 + 15)
        rimbuf[...] = (dot(last_x, xsel[3].astype(BF16)) + dot(last_m, midb[...])).astype(BF16)
        remote(rimbuf, rim_a, rs.at[2], rr.at[2], follow).start()
        pl.when(has_over)(lambda: remote(rimbuf, rim_b, rs.at[3], rr.at[3], over).start())

    def pool_second():
        remote(rimbuf, rim_a, rs.at[2], rr.at[2], follow).wait_recv()
        pl.when(has_under)(lambda: remote(rimbuf, rim_b, rs.at[3], rr.at[3], under).wait_recv())
        shift = jnp.where(head, 1, 0)
        step_back = one_hot((M, M), lambda row, col: jnp.logical_and(row % 16 != 0, col == row - 1))

        def rim_of(base):
            def from_a(row, col):
                k = row // 16 - shift
                return jnp.logical_and(row % 16 == 0, jnp.logical_and(k >= 0, col == base + k))

            def from_b(row, col):
                return jnp.logical_and(row == 0, col == base + POS - 1)

            return dot(one_hot((M, 16), from_a), rim_a[...]) + dot(one_hot((M, 16), from_b), rim_b[...])

        x_back = dot(step_back, xsel[3].astype(BF16)) + rim_of(0)
        mid_back = dot(step_back, midb[...]) + rim_of(POS)
        mid_even = (pool1[0:1] * x_back + pool1[1:2] * xsel[0] + pool1[2:3] * xsel[1]).astype(BF16)
        pooled = pool2[0:1] * mid_back + pool2[1:2] * mid_even.astype(F32) + pool2[2:3] * midb[...].astype(F32)
        pbuf[...] = pooled.astype(BF16).reshape(POS, 16, C)
        for step in range(1, POS):
            p_send((me + step) % POS).start()
        p_local().start()

    def pipeline(t, carry):
        pl.when(t >= 4)(lambda: stage_e(t - 4))
        pl.when(jnp.logical_and(t >= 3, t < SUB + 3))(lambda: stage_d(t - 3))
        pl.when(jnp.logical_and(t >= 2, t < SUB + 2))(lambda: stage_c(t - 2))
        pl.when(jnp.logical_and(t >= 1, t < SUB + 1))(lambda: stage_b(t - 1))
        pl.when(t < SUB)(lambda: stage_a(t))
        pl.when(t == SUB + 1)(pool_first)
        pl.when(t == SUB + 2)(pool_second)
        return carry

    lax.fori_loop(0, SUB + 4, pipeline, 0)

    for step in range(1, POS):
        j = (me + step) % POS
        g_send(j).wait_send()
        p_send(j).wait_send()
        p_recv(j).wait_recv()
    p_local().wait()

    def drain(s, carry):
        for step in range(1, POS):
            j = (me + step) % POS
            x_send(j, s).wait_send()
            o_send(j, s).wait_send()
            o_recv(j, s).wait_recv()
        o_local(s).wait()
        for kind, (buf, reach) in enumerate(halos):
            pl.when(jnp.logical_not(first))(lambda: halo_down(kind, buf, reach, s).wait_send())
            pl.when(jnp.logical_not(last))(lambda: halo_up(kind, buf, reach, s).wait_send())
        return carry

    lax.fori_loop(0, SUB, drain, 0)
    remote(grimbuf, grim_a, rs.at[0], rr.at[0], before).wait_send()
    remote(rimbuf, rim_a, rs.at[2], rr.at[2], follow).wait_send()
    pl.when(has_under)(lambda: remote(grimbuf, grim_b, rs.at[1], rr.at[1], under).wait_send())
    pl.when(has_over)(lambda: remote(rimbuf, rim_b, rs.at[3], rr.at[3], over).wait_send())


def body(
    sequence_input, first_depthwise_taps, first_norm_gain, first_up_weight, first_down_weight,
    second_depthwise_taps, second_norm_gain, second_up_weight, second_down_weight,
    pool_one, pool_two, pooled_cotangent,
):
    whole = pl.BlockSpec(memory_space=pltpu.VMEM)
    there = pl.BlockSpec(memory_space=pl.ANY)
    dma = pltpu.SemaphoreType.DMA
    rim = pltpu.VMEM((16, C), BF16)
    return pl.pallas_call(
        kernel,
        out_shape=(
            jax.ShapeDtypeStruct(pooled_cotangent.shape, BF16),
            jax.ShapeDtypeStruct(sequence_input.shape, BF16),
        ),
        in_specs=[there, whole, whole, there, there, whole, whole, there, there, whole, whole, there],
        out_specs=(there, there),
        scratch_shapes=[
            pltpu.VMEM((SUB, POS + 2, ROWS, C), BF16),
            pltpu.VMEM((SUB, POS + 8, ROWS, C), BF16),
            pltpu.VMEM((SUB, POS + 8, ROWS, C), BF16),
            pltpu.VMEM((SUB, POS + 2, ROWS, C), BF16),
            pltpu.VMEM((POS, 16, C), BF16),
            rim, rim, rim, rim, rim, rim,
            pltpu.VMEM((SUB, M, C), F32),
            pltpu.VMEM((SUB, M, 1), F32),
            pltpu.VMEM((SUB, M, HID), F32),
            pltpu.VMEM((SUB, M, C), F32),
            pltpu.VMEM((SUB, M, C), F32),
            pltpu.VMEM((SUB, M, C), BF16),
            pltpu.VMEM((SUB, POS, ROWS, C), BF16),
            pltpu.VMEM((POS, 16, C), BF16),
            pltpu.VMEM((4, M, C), F32),
            pltpu.VMEM((M, C), BF16),
            pltpu.VMEM((C, HID), BF16), pltpu.VMEM((HID, C), BF16),
            pltpu.VMEM((C, HID), BF16), pltpu.VMEM((HID, C), BF16),
            pltpu.VMEM((HID, C), BF16), pltpu.VMEM((C, HID), BF16),
            pltpu.VMEM((HID, C), BF16), pltpu.VMEM((C, HID), BF16),
            dma((SUB, POS)), dma((SUB, POS)),
            dma((POS,)), dma((POS,)),
            dma((4, SUB, 2)), dma((4, SUB, 2)),
            dma((SUB, POS)), dma((SUB, POS)),
            dma((POS,)), dma((POS,)),
            dma((4,)), dma((4,)),
            dma((4,)), dma((1,)),
        ],
        compiler_params=pltpu.CompilerParams(
            collective_id=0, has_side_effects=True, vmem_limit_bytes=48 * 2**20
        ),
        cost_estimate=pl.CostEstimate(flops=4300000000, bytes_accessed=8000000, transcendentals=1000000),
    )(
        sequence_input, first_depthwise_taps, first_norm_gain.reshape(1, C), first_up_weight, first_down_weight,
        second_depthwise_taps, second_norm_gain.reshape(1, C), second_up_weight, second_down_weight,
        pool_one, pool_two, pooled_cotangent,
    )


def solution(mesh):
    split = P(None, ("major", "minor"), None)
    return jax.shard_map(
        body,
        mesh=mesh,
        in_specs=(split,) + (P(),) * 10 + (split,),
        out_specs=(split, split),
        check_vma=False,
    )
```

time: 367 us -> 111 us (0.30)
  the two profiles are of different devices: /device:TPU:34 before, /device:TPU:57 now
where the time goes in v1:
time: 111 us; the launch traced here: 110 us
  Pallas kernels  97.2 us (88%)
  local copies, waits for them, and re-layouts  12.4 us (11%)
    pallas_call x1, Pallas kernels, body(): pl.pallas_call(kernel, out_shape=(jax.ShapeDtypeStruct(pooled_cotangent.s...  97.2 us
    unnamed x26, local copies, waits for them, and re-layouts  12.4 us

profile of v1, /device:TPU:57, one launch (start us, length us, event | category | flops | bytes accessed | tf_op | source)
XLA Modules:
  0.0 110.3 jit_solution(10875723236687631016)
XLA Ops:
  0.6 0.0 copy-start.10
  0.6 0.7 copy-done.10
  1.3 0.0 copy-start
  1.3 1.2 %copy-done = bf16[512,1024]{1,0:T(8,128)(2,1)S(1)} copy-done((bf16[512,1024]{1,0:T(8,128)(2,1)S(1)}, bf16[512,1024]{1,0:T(8,128)(2,1)}, u32[]{:S(2)}) %copy-start) | copy-done | bytes 1048600
  2.5 0.0 copy-start.1
  2.5 1.2 %copy-done.1 = bf16[1024,512]{1,0:T(8,128)(2,1)S(1)} copy-done((bf16[1024,512]{1,0:T(8,128)(2,1)S(1)}, bf16[1024,512]{1,0:T(8,128)(2,1)}, u32[]{:S(2)}) %copy-start.1) | copy-done | bytes 1048600
  3.8 0.0 copy-start.2
  3.8 1.2 %copy-done.2 = bf16[512,1024]{1,0:T(8,128)(2,1)S(1)} copy-done((bf16[512,1024]{1,0:T(8,128)(2,1)S(1)}, bf16[512,1024]{1,0:T(8,128)(2,1)}, u32[]{:S(2)}) %copy-start.2) | copy-done | bytes 1048600
  5.0 0.0 copy-start.3
  5.0 1.2 %copy-done.3 = bf16[1024,512]{1,0:T(8,128)(2,1)S(1)} copy-done((bf16[1024,512]{1,0:T(8,128)(2,1)S(1)}, bf16[1024,512]{1,0:T(8,128)(2,1)}, u32[]{:S(2)}) %copy-start.3) | copy-done | bytes 1048600
  6.2 0.0 copy-start.4
  6.2 1.0 copy-done.4
  7.3 0.0 copy-start.5
  7.3 0.9 copy-done.5
  8.2 0.0 copy-start.6
  8.2 0.7 copy-done.6
  8.9 0.0 copy-start.7
  8.9 0.7 copy-done.7
  9.6 0.0 copy-start.8
  9.6 0.7 copy-done.8
  10.3 0.0 copy-start.9
  10.3 0.7 copy-done.9
  11.0 0.0 copy-start.11
  11.0 0.7 copy-done.11
  11.6 97.2 %shard_map.131 = (bf16[4,32,512]{2,1,0:T(8,128)(2,1)S(1)}, bf16[4,128,512]{2,1,0:T(8,128)(2,1)S(1)}) custom-call(bf16[4,128,512]{2,1,0:T(8,128)(2,1)S(1)} %copy-done.4, f32[3,512]{1,0:T(4,128)S(1)} %copy-done.6, f32[1,512]{1,0:T(1,128)S(1)} %bitcast.2, bf16[512,1024]{1,0:T(8,128)(2,1)S(1)} %copy-done, bf16[1024,512]{1,0:T(8,128)(2,1)S(1)} %copy-done.1, ...), custom_call_target="tpu_custom_call" | custom-call | flops 4300000256 | bytes 8000000 | tf_op jit(solution)/shard_map/pallas_call | solution.py:417
  108.9 0.7 copy.16
  109.5 0.8 copy.17
Async XLA Ops:
  0.6 0.7 copy-start.10
  1.3 1.2 %copy-start = (bf16[512,1024]{1,0:T(8,128)(2,1)S(1)}, bf16[512,1024]{1,0:T(8,128)(2,1)}, u32[]{:S(2)}) copy-start(bf16[512,1024]{1,0:T(8,128)(2,1)} %up1_hbm.1) | copy-start | bytes 3145732
  2.5 1.2 %copy-start.1 = (bf16[1024,512]{1,0:T(8,128)(2,1)S(1)}, bf16[1024,512]{1,0:T(8,128)(2,1)}, u32[]{:S(2)}) copy-start(bf16[1024,512]{1,0:T(8,128)(2,1)} %down1_hbm.1) | copy-start | bytes 3145732
  3.8 1.2 %copy-start.2 = (bf16[512,1024]{1,0:T(8,128)(2,1)S(1)}, bf16[512,1024]{1,0:T(8,128)(2,1)}, u32[]{:S(2)}) copy-start(bf16[512,1024]{1,0:T(8,128)(2,1)} %up2_hbm.1) | copy-start | bytes 3145732
  5.0 1.2 %copy-start.3 = (bf16[1024,512]{1,0:T(8,128)(2,1)S(1)}, bf16[1024,512]{1,0:T(8,128)(2,1)}, u32[]{:S(2)}) copy-start(bf16[1024,512]{1,0:T(8,128)(2,1)} %down2_hbm.1) | copy-start | bytes 3145732
  6.2 1.0 copy-start.4
  7.3 0.9 copy-start.5
  8.2 0.7 copy-start.6
  8.9 0.7 copy-start.7
  9.6 0.7 copy-start.8
  10.3 0.7 copy-start.9
  11.0 0.7 copy-start.11

commit v2 on v1

--- a/solution.py
+++ b/solution.py
@@ -17,6 +17,7 @@
 ROWS = 16
 CHUNK = SUB * ROWS
 M = POS * ROWS
+VMEM_BYTES = 60 * 2**20
 GELU_A = 0.7978845608028654
 GELU_B = 0.044715
 
@@ -44,12 +45,12 @@
 
 
 def kernel(
-    x_ref, taps1, gain1, up1_hbm, down1_hbm, taps2, gain2, up2_hbm, down2_hbm, pool1, pool2, g_ref,
+    x_ref, taps1_hbm, gain1_hbm, up1_hbm, down1_hbm, taps2_hbm, gain2_hbm, up2_hbm, down2_hbm, pool1_hbm, pool2_hbm, g_ref,
     pooled_ref, out_ref,
     xbuf, x1buf, gc2buf, gc1buf, gbuf, grimbuf, grim_a, grim_b, rimbuf, rim_a, rim_b,
     conv1, scale1, slope1, gy2, gy1, x2buf, obuf, pbuf, xsel, midb,
-    up1, down1, up2, down2, up1t, down1t, up2t, down2t,
-    xs, xr, gs, gr, hs, hr, os, orr, ps, pr, rs, rr, ws, loc,
+    taps1, gain1, up1, down1, taps2, gain2, up2, down2, pool1, pool2, up1t, down1t, up2t, down2t,
+    xs, xr, gs, gr, hs, hr, os, orr, ps, pr, rs, rr, ws,
 ):
     major, minor = lax.axis_index("major"), lax.axis_index("minor")
     zhi, x = minor // 4, minor % 4
@@ -81,13 +82,16 @@
     pl.when(jnp.logical_and(tail, jnp.logical_not(last)))(lambda: greet(over))
     pl.when(jnp.logical_and(head, jnp.logical_not(first)))(lambda: greet(under))
 
-    weight_copies = [
+    parameter_copies = [
         pltpu.make_async_copy(source, target, ws.at[k])
         for k, (source, target) in enumerate(
-            ((up1_hbm, up1), (down1_hbm, down1), (up2_hbm, up2), (down2_hbm, down2))
+            (
+                (taps1_hbm, taps1), (gain1_hbm, gain1), (up1_hbm, up1), (down1_hbm, down1), (taps2_hbm, taps2),
+                (gain2_hbm, gain2), (up2_hbm, up2), (down2_hbm, down2), (pool1_hbm, pool1), (pool2_hbm, pool2),
+            )
         )
     ]
-    for copy in weight_copies:
+    for copy in parameter_copies:
         copy.start()
 
     def remote(source, target, send, recv, device):
@@ -208,7 +212,7 @@
     send_x(2)
     send_x(3)
 
-    for copy in weight_copies:
+    for copy in parameter_copies:
         copy.wait()
     up1t[...] = up1[...].T
     down1t[...] = down1[...].T
@@ -410,17 +414,17 @@
     second_depthwise_taps, second_norm_gain, second_up_weight, second_down_weight,
     pool_one, pool_two, pooled_cotangent,
 ):
-    whole = pl.BlockSpec(memory_space=pltpu.VMEM)
     there = pl.BlockSpec(memory_space=pl.ANY)
     dma = pltpu.SemaphoreType.DMA
     rim = pltpu.VMEM((16, C), BF16)
+    three, one = pltpu.VMEM((3, C), F32), pltpu.VMEM((1, C), F32)
     return pl.pallas_call(
         kernel,
         out_shape=(
             jax.ShapeDtypeStruct(pooled_cotangent.shape, BF16),
             jax.ShapeDtypeStruct(sequence_input.shape, BF16),
         ),
-        in_specs=[there, whole, whole, there, there, whole, whole, there, there, whole, whole, there],
+        in_specs=[there] * 12,
         out_specs=(there, there),
         scratch_shapes=[
             pltpu.VMEM((SUB, POS + 2, ROWS, C), BF16),
@@ -439,8 +443,9 @@
             pltpu.VMEM((POS, 16, C), BF16),
             pltpu.VMEM((4, M, C), F32),
             pltpu.VMEM((M, C), BF16),
-            pltpu.VMEM((C, HID), BF16), pltpu.VMEM((HID, C), BF16),
-            pltpu.VMEM((C, HID), BF16), pltpu.VMEM((HID, C), BF16),
+            three, one, pltpu.VMEM((C, HID), BF16), pltpu.VMEM((HID, C), BF16),
+            three, one, pltpu.VMEM((C, HID), BF16), pltpu.VMEM((HID, C), BF16),
+            three, three,
             pltpu.VMEM((HID, C), BF16), pltpu.VMEM((C, HID), BF16),
             pltpu.VMEM((HID, C), BF16), pltpu.VMEM((C, HID), BF16),
             dma((SUB, POS)), dma((SUB, POS)),
@@ -449,10 +454,10 @@
             dma((SUB, POS)), dma((SUB, POS)),
             dma((POS,)), dma((POS,)),
             dma((4,)), dma((4,)),
-            dma((4,)), dma((1,)),
+            dma((10,)),
         ],
         compiler_params=pltpu.CompilerParams(
-            collective_id=0, has_side_effects=True, vmem_limit_bytes=48 * 2**20
+            collective_id=0, has_side_effects=True, vmem_limit_bytes=VMEM_BYTES
         ),
         cost_estimate=pl.CostEstimate(flops=4300000000, bytes_accessed=8000000, transcendentals=1000000),
     )(

time: 111 us -> 102 us (0.919)
  local copies, waits for them, and re-layouts: 12.4 us -> 3.44 us
    unnamed x26 -> x2, local copies, waits for them, and re-layouts: 12.4 us -> 3.44 us
where the time goes in v2:
time: 102 us
  Pallas kernels  97.9 us (96%)
  local copies, waits for them, and re-layouts  3.44 us (3%)
    pallas_call x1, Pallas kernels, body(): pl.pallas_call(kernel, out_shape=(jax.ShapeDtypeStruct(pooled_cotangent.s...  97.9 us
    unnamed x2, local copies, waits for them, and re-layouts  3.44 us

profile of v2, /device:TPU:57, one launch (start us, length us, event | category | flops | bytes accessed | tf_op | source)
XLA Modules:
  0.0 101.9 jit_solution(105626904327178103)
XLA Ops:
  0.6 97.9 %shard_map.131 = (bf16[4,32,512]{2,1,0:T(8,128)(2,1)}, bf16[4,128,512]{2,1,0:T(8,128)(2,1)}) custom-call(bf16[4,128,512]{2,1,0:T(8,128)(2,1)} %x_ref.1, f32[3,512]{1,0:T(4,128)} %taps1_hbm.1, f32[1,512]{1,0:T(1,128)} %bitcast.2, bf16[512,1024]{1,0:T(8,128)(2,1)} %up1_hbm.1, bf16[1024,512]{1,0:T(8,128)(2,1)} %down1_hbm.1, f32[3,512]{1,0:T(4,128)} %taps2_hbm.1, ...), custom_call_target="tpu_custom_call" | custom-call | flops 4300000256 | bytes 8000000 | tf_op jit(solution)/shard_map/pallas_call | solution.py:421
  98.5 1.6 %copy.16 = bf16[4,32,512]{2,1,0:T(8,128)(2,1)} copy(bf16[4,32,512]{2,1,0:T(8,128)(2,1)} %get-tuple-element.4) | data formatting | bytes 262144
  100.1 1.9 %copy.17 = bf16[4,128,512]{2,1,0:T(8,128)(2,1)} copy(bf16[4,128,512]{2,1,0:T(8,128)(2,1)} %get-tuple-element.5) | data formatting | bytes 1048576

commit v3 on v2

--- a/solution.py
+++ b/solution.py
@@ -17,6 +17,10 @@
 ROWS = 16
 CHUNK = SUB * ROWS
 M = POS * ROWS
+REACH = 5
+WIDE = POS + 2 * REACH
+NEAR = POS + 2
+MN = NEAR * ROWS
 VMEM_BYTES = 60 * 2**20
 GELU_A = 0.7978845608028654
 GELU_B = 0.044715
@@ -36,19 +40,19 @@
     return value.reshape(-1, C)
 
 
-def gelu_parts(a):
-    square = a * a
-    t = jnp.tanh(GELU_A * a * (1.0 + GELU_B * square))
-    half = 0.5 + 0.5 * t
-    slope = half + 0.5 * a * (1.0 - t * t) * (GELU_A * (1.0 + 3.0 * GELU_B * square))
-    return a * half, slope
+def gelu_tanh(a):
+    return jnp.tanh(GELU_A * a * (1.0 + GELU_B * (a * a)))
+
+
+def gelu_slope(a, t):
+    return 0.5 + 0.5 * t + 0.5 * a * (1.0 - t * t) * (GELU_A * (1.0 + 3.0 * GELU_B * (a * a)))
 
 
 def kernel(
     x_ref, taps1_hbm, gain1_hbm, up1_hbm, down1_hbm, taps2_hbm, gain2_hbm, up2_hbm, down2_hbm, pool1_hbm, pool2_hbm, g_ref,
     pooled_ref, out_ref,
     xbuf, x1buf, gc2buf, gc1buf, gbuf, grimbuf, grim_a, grim_b, rimbuf, rim_a, rim_b,
-    conv1, scale1, slope1, gy2, gy1, x2buf, obuf, pbuf, xsel, midb,
+    conv1, scale1, slope1, gy2, x2buf, obuf, pbuf, xsel, midb,
     taps1, gain1, up1, down1, taps2, gain2, up2, down2, pool1, pool2, up1t, down1t, up2t, down2t,
     xs, xr, gs, gr, hs, hr, os, orr, ps, pr, rs, rr, ws,
 ):
@@ -104,25 +108,25 @@
         return x_ref.at[j // 2, pl.ds((j % 2) * CHUNK + s * ROWS, ROWS)]
 
     def x_send(j, s):
-        return remote(x_rows(j, s), xbuf.at[s, 1 + me], xs.at[s, j], xr.at[s, me], member(j))
+        return remote(x_rows(j, s), xbuf.at[s, REACH + me], xs.at[s, j], xr.at[s, me], member(j))
 
     def x_recv(j, s):
-        return remote(x_rows(j, s), xbuf.at[s, 1 + j], xs.at[s, j], xr.at[s, j], member(j))
+        return remote(x_rows(j, s), xbuf.at[s, REACH + j], xs.at[s, j], xr.at[s, j], member(j))
 
     def x_local(s):
-        return pltpu.make_async_copy(x_rows(me, s), xbuf.at[s, 1 + me], xr.at[s, me])
+        return pltpu.make_async_copy(x_rows(me, s), xbuf.at[s, REACH + me], xr.at[s, me])
 
     def g_rows(j):
         return g_ref.at[j // 2, pl.ds((j % 2) * 16, 16)]
 
     def g_send(j):
-        return remote(g_rows(j), gbuf.at[me], gs.at[j], gr.at[me], member(j))
+        return remote(g_rows(j), gbuf.at[1 + me], gs.at[j], gr.at[me], member(j))
 
     def g_recv(j):
-        return remote(g_rows(j), gbuf.at[j], gs.at[j], gr.at[j], member(j))
+        return remote(g_rows(j), gbuf.at[1 + j], gs.at[j], gr.at[j], member(j))
 
     def g_local():
-        return pltpu.make_async_copy(g_rows(me), gbuf.at[me], gr.at[me])
+        return pltpu.make_async_copy(g_rows(me), gbuf.at[1 + me], gr.at[me])
 
     def out_rows(s):
         return out_ref.at[zhi, pl.ds(half * CHUNK + s * ROWS, ROWS)]
@@ -150,14 +154,13 @@
 
     def halo_down(kind, buf, reach, s):
         return remote(
-            buf.at[s, pl.ds(reach, reach)], buf.at[s, pl.ds(reach + POS, reach)],
+            buf.at[pl.ds(reach, reach)], buf.at[pl.ds(reach + POS, reach)],
             hs.at[kind, s, 0], hr.at[kind, s, 0], below,
         )
 
     def halo_up(kind, buf, reach, s):
         return remote(
-            buf.at[s, pl.ds(POS, reach)], buf.at[s, pl.ds(0, reach)],
-            hs.at[kind, s, 1], hr.at[kind, s, 1], above,
+            buf.at[pl.ds(POS, reach)], buf.at[pl.ds(0, reach)], hs.at[kind, s, 1], hr.at[kind, s, 1], above,
         )
 
     def send_halos(kind, buf, reach, s):
@@ -168,18 +171,23 @@
         pl.when(jnp.logical_not(last))(lambda: halo_down(kind, buf, reach, s).wait_recv())
         pl.when(jnp.logical_not(first))(lambda: halo_up(kind, buf, reach, s).wait_recv())
 
-    halos = ((xbuf, 1), (x1buf, 4), (gc2buf, 4), (gc1buf, 1))
-
-    for buf, reach in halos:
-        zeros = jnp.zeros((SUB, reach, ROWS, C), BF16)
-
-        @pl.when(first)
-        def _(buf=buf, reach=reach, zeros=zeros):
-            buf[:, pl.ds(0, reach)] = zeros
-
-        @pl.when(last)
-        def _(buf=buf, reach=reach, zeros=zeros):
-            buf[:, pl.ds(reach + POS, reach)] = zeros
+    def end_halos(kind, buf, reach, s):
+        pl.when(jnp.logical_not(first))(lambda: halo_down(kind, buf, reach, s).wait_send())
+        pl.when(jnp.logical_not(last))(lambda: halo_up(kind, buf, reach, s).wait_send())
+
+    zeros = jnp.zeros((SUB, REACH, ROWS, C), BF16)
+
+    @pl.when(first)
+    def _():
+        xbuf[:, pl.ds(0, REACH)] = zeros
+        gc2buf[:, pl.ds(0, REACH)] = zeros
+        gbuf[0] = zeros[0, 0]
+
+    @pl.when(last)
+    def _():
+        xbuf[:, pl.ds(REACH + POS, REACH)] = zeros
+        gc2buf[:, pl.ds(REACH + POS, REACH)] = zeros
+        gbuf[1 + POS] = zeros[0, 0]
 
     has_under = jnp.logical_and(head, jnp.logical_not(first))
     has_over = jnp.logical_and(tail, jnp.logical_not(last))
@@ -204,11 +212,14 @@
             x_send((me + step) % POS, s).start()
         x_local(s).start()
 
+    def send_g():
+        for step in range(1, POS):
+            g_send((me + step) % POS).start()
+        g_local().start()
+
     send_x(0)
     send_x(1)
-    for step in range(1, POS):
-        g_send((me + step) % POS).start()
-    g_local().start()
+    send_g()
     send_x(2)
     send_x(3)
 
@@ -219,16 +230,19 @@
     up2t[...] = up2[...].T
     down2t[...] = down2[...].T
 
-    def forward(buf, reach, s, taps, gain, up, down):
-        lowered = rows_of(buf[s, pl.ds(0, POS)]).astype(F32)
-        here = rows_of(buf[s, pl.ds(reach, POS)]).astype(F32)
-        raised = rows_of(buf[s, pl.ds(2 * reach, POS)]).astype(F32)
+    def three_of(buf, reach, count):
+        return [rows_of(buf[pl.ds(k * reach, count)]).astype(F32) for k in range(3)]
+
+    def forward(buf, reach, count, taps, gain, up, down):
+        lowered, here, raised = three_of(buf, reach, count)
         conv = taps[0:1] * lowered + taps[1:2] * here + taps[2:3] * raised
         scale = lax.rsqrt(jnp.mean(conv * conv, -1, keepdims=True) + 1e-06)
         normed = (conv * scale * gain[...]).astype(BF16)
-        hidden, slope = gelu_parts(dot(normed, up[...]))
-        out = (here + dot(hidden.astype(BF16), down[...])).astype(BF16)
-        return out, conv, scale, slope
+        a = dot(normed, up[...])
+        t = gelu_tanh(a)
+        hidden = (a * (0.5 + 0.5 * t)).astype(BF16)
+        out = (here + dot(hidden, down[...])).astype(BF16)
+        return out, conv, scale, a, t
 
     def backward(grad, conv, scale, slope, gain, upt, downt):
         grad_pre = (slope * dot(grad.astype(BF16), downt[...])).astype(BF16)
@@ -236,92 +250,114 @@
         mean = jnp.mean(scaled * conv, -1, keepdims=True)
         return (scale * scaled - conv * (scale * scale * scale) * mean).astype(BF16)
 
-    def spread(grad, buf, reach, s, taps):
-        lowered = rows_of(buf[s, pl.ds(0, POS)]).astype(F32)
-        here = rows_of(buf[s, pl.ds(reach, POS)]).astype(F32)
-        raised = rows_of(buf[s, pl.ds(2 * reach, POS)]).astype(F32)
+    def spread(grad, buf, reach, count, taps):
+        lowered, here, raised = three_of(buf, reach, count)
         return grad + taps[0:1] * raised + taps[1:2] * here + taps[2:3] * lowered
 
-    def top_coefficients():
+    def top_coefficients(rows):
         one, two = [pool1[k : k + 1] for k in range(3)], [pool2[k : k + 1] for k in range(3)]
         here = (one[1] * two[1], one[2] * two[1] + one[0] * two[2], one[1] * two[2], one[2] * two[2])
         ahead = (jnp.zeros((1, C), F32), one[0] * two[0], one[1] * two[0], one[2] * two[0] + one[0] * two[1])
-        place = lax.broadcasted_iota(jnp.int32, (M, C), 0) % 4
+        place = lax.broadcasted_iota(jnp.int32, (rows, C), 0) % 4
 
         def pick(four):
             return jnp.where(place == 0, four[0], jnp.where(place == 1, four[1], jnp.where(place == 2, four[2], four[3])))
 
         return pick(here), pick(ahead)
 
-    def stage_a(s):
-        for step in range(1, POS):
-            x_recv((me + step) % POS, s).wait_recv()
-        x_local(s).wait()
-        send_halos(0, xbuf, 1, s)
-
-    def stage_b(s):
-        wait_halos(0, xbuf, 1, s)
-        out, conv, scale, slope = forward(xbuf, 1, s, taps1, gain1, up1, down1)
-        x1buf[s, pl.ds(4, POS)] = out.reshape(POS, ROWS, C)
-        send_halos(1, x1buf, 4, s)
-        conv1[s] = conv
-        scale1[s] = scale
-        slope1[s] = slope
-
     def take_g():
         for step in range(1, POS):
             g_recv((me + step) % POS).wait_recv()
         g_local().wait()
-        firsts = one_hot((16, M), lambda row, col: jnp.logical_and(col == row * 16, row < POS))
+        send_halos(2, gbuf, 1, 0)
+
+    def share_g():
+        wait_halos(2, gbuf, 1, 0)
+        firsts = one_hot((16, MN), lambda row, col: jnp.logical_and(col == row * 16, row < NEAR))
         grimbuf[...] = dot(firsts, rows_of(gbuf[...])).astype(BF16)
         remote(grimbuf, grim_a, rs.at[0], rr.at[0], before).start()
         pl.when(has_under)(lambda: remote(grimbuf, grim_b, rs.at[1], rr.at[1], under).start())
 
-    def stage_c(s):
-        pl.when(s == 0)(take_g)
-        coef_here, coef_ahead = top_coefficients()
-        g_all = rows_of(gbuf[...])
+    def take_g_rims():
+        remote(grimbuf, grim_a, rs.at[0], rr.at[0], before).wait_recv()
+        pl.when(has_over)(lambda: remote(grimbuf, grim_b, rs.at[1], rr.at[1], over).wait_recv())
+
+    def grad_top(s, start, count):
+        rows = count * ROWS
+        place = pl.ds(start * ROWS, rows)
+        coef_here, coef_ahead = top_coefficients(rows)
+        g_all = rows_of(gbuf[pl.ds(start, count)])
 
         def take(row, col, ahead):
             return jnp.logical_and(row // ROWS == col // 16, (row % ROWS) // 4 + ahead + 4 * s == col % 16)
 
-        here = dot(one_hot((M, M), lambda row, col: take(row, col, 0)), g_all)
-        ahead = dot(one_hot((M, M), lambda row, col: take(row, col, 1)), g_all)
-        gy2[s] = coef_here * here + coef_ahead * ahead
+        here = dot(one_hot((rows, rows), lambda row, col: take(row, col, 0)), g_all)
+        ahead = dot(one_hot((rows, rows), lambda row, col: take(row, col, 1)), g_all)
+        gy2[place] = coef_here * here + coef_ahead * ahead
 
         @pl.when(s == SUB - 1)
         def _():
-            remote(grimbuf, grim_a, rs.at[0], rr.at[0], before).wait_recv()
-            pl.when(has_over)(lambda: remote(grimbuf, grim_b, rs.at[1], rr.at[1], over).wait_recv())
             shift = jnp.where(tail, 1, 0)
 
+            def end(row):
+                return row % ROWS >= ROWS - 4
+
             def from_a(row, col):
-                return jnp.logical_and(row % ROWS >= ROWS - 4, jnp.logical_and(row // ROWS + shift == col, col < POS))
+                return jnp.logical_and(end(row), jnp.logical_and(row // ROWS + start + shift == col, col < NEAR))
 
             def from_b(row, col):
-                return jnp.logical_and(row >= M - 4, col == 0)
-
-            rim = dot(one_hot((M, 16), from_a), grim_a[...]) + dot(one_hot((M, 16), from_b), grim_b[...])
-            gy2[s] = gy2[s] + coef_ahead * rim
-
-        wait_halos(1, x1buf, 4, s)
-        out, conv, scale, slope = forward(x1buf, 4, s, taps2, gain2, up2, down2)
+                return jnp.logical_and(end(row), jnp.logical_and(row // ROWS + start == NEAR - 1, col == 2))
+
+            rim = dot(one_hot((rows, 16), from_a), grim_a[...]) + dot(one_hot((rows, 16), from_b), grim_b[...])
+            gy2[place] = gy2[place] + coef_ahead * rim
+
+    def stage_a(s):
+        for step in range(1, POS):
+            x_recv((me + step) % POS, s).wait_recv()
+        x_local(s).wait()
+        send_halos(0, xbuf.at[s], REACH, s)
+
+    def stage_b(s):
+        wait_halos(0, xbuf.at[s], REACH, s)
+        out, conv, scale, a, t = forward(xbuf.at[s], 1, POS + 8, taps1, gain1, up1, down1)
+        x1buf[...] = out.reshape(POS + 8, ROWS, C)
+        near = slice(3 * ROWS, 3 * ROWS + MN)
+        conv1[s] = conv[near]
+        scale1[s] = scale[near]
+        slope1[s] = gelu_slope(a[near], t[near])
+
+        @pl.when(first)
+        def _():
+            x1buf[pl.ds(0, 4)] = jnp.zeros((4, ROWS, C), BF16)
+
+        @pl.when(last)
+        def _():
+            x1buf[pl.ds(4 + POS, 4)] = jnp.zeros((4, ROWS, C), BF16)
+
+        grad_top(s, 1, POS)
+        out, conv, scale, a, t = forward(x1buf, 4, POS, taps2, gain2, up2, down2)
         x2buf[s] = out
-        grad_conv = backward(gy2[s], conv, scale, slope, gain2, up2t, down2t)
-        gc2buf[s, pl.ds(4, POS)] = grad_conv.reshape(POS, ROWS, C)
-        send_halos(2, gc2buf, 4, s)
-
-    def stage_d(s):
-        wait_halos(2, gc2buf, 4, s)
-        grad = spread(gy2[s], gc2buf, 4, s, taps2)
+        grad_conv = backward(gy2[pl.ds(ROWS, M)], conv, scale, gelu_slope(a, t), gain2, up2t, down2t)
+        gc2buf[s, pl.ds(REACH, POS)] = grad_conv.reshape(POS, ROWS, C)
+        send_halos(1, gc2buf.at[s], REACH, s)
+
+    def stage_c(s):
+        wait_halos(1, gc2buf.at[s], REACH, s)
+        grad_top(s, 0, NEAR)
+        grad = spread(gy2[...], gc2buf.at[s], 4, NEAR, taps2)
         grad_conv = backward(grad, conv1[s], scale1[s], slope1[s], gain1, up1t, down1t)
-        gc1buf[s, pl.ds(1, POS)] = grad_conv.reshape(POS, ROWS, C)
-        send_halos(3, gc1buf, 1, s)
-        gy1[s] = grad
-
-    def stage_e(s):
-        wait_halos(3, gc1buf, 1, s)
-        obuf[s] = spread(gy1[s], gc1buf, 1, s, taps1).astype(BF16).reshape(POS, ROWS, C)
+        gc1buf[...] = grad_conv.reshape(NEAR, ROWS, C)
+
+        @pl.when(first)
+        def _():
+            gc1buf[0] = jnp.zeros((ROWS, C), BF16)
+
+        @pl.when(last)
+        def _():
+            gc1buf[NEAR - 1] = jnp.zeros((ROWS, C), BF16)
+
+        result = spread(grad[ROWS : ROWS + M], gc1buf, 1, POS, taps1)
+        obuf[s] = result.astype(BF16).reshape(POS, ROWS, C)
         for step in range(1, POS):
             o_send((me + step) % POS, s).start()
         o_local(s).start()
@@ -372,16 +408,17 @@
         p_local().start()
 
     def pipeline(t, carry):
-        pl.when(t >= 4)(lambda: stage_e(t - 4))
-        pl.when(jnp.logical_and(t >= 3, t < SUB + 3))(lambda: stage_d(t - 3))
-        pl.when(jnp.logical_and(t >= 2, t < SUB + 2))(lambda: stage_c(t - 2))
-        pl.when(jnp.logical_and(t >= 1, t < SUB + 1))(lambda: stage_b(t - 1))
         pl.when(t < SUB)(lambda: stage_a(t))
-        pl.when(t == SUB + 1)(pool_first)
-        pl.when(t == SUB + 2)(pool_second)
+        pl.when(t == 1)(take_g)
+        pl.when(t == 2)(share_g)
+        pl.when(t == SUB)(take_g_rims)
+        pl.when(jnp.logical_and(t >= 1, t <= SUB))(lambda: stage_b(t - 1))
+        pl.when(t == SUB + 1)(pool_second)
+        pl.when(t >= 2)(lambda: stage_c(t - 2))
+        pl.when(t == SUB)(pool_first)
         return carry
 
-    lax.fori_loop(0, SUB + 4, pipeline, 0)
+    lax.fori_loop(0, SUB + 2, pipeline, 0)
 
     for step in range(1, POS):
         j = (me + step) % POS
@@ -397,12 +434,12 @@
             o_send(j, s).wait_send()
             o_recv(j, s).wait_recv()
         o_local(s).wait()
-        for kind, (buf, reach) in enumerate(halos):
-            pl.when(jnp.logical_not(first))(lambda: halo_down(kind, buf, reach, s).wait_send())
-            pl.when(jnp.logical_not(last))(lambda: halo_up(kind, buf, reach, s).wait_send())
+        end_halos(0, xbuf.at[s], REACH, s)
+        end_halos(1, gc2buf.at[s], REACH, s)
         return carry
 
     lax.fori_loop(0, SUB, drain, 0)
+    end_halos(2, gbuf, 1, 0)
     remote(grimbuf, grim_a, rs.at[0], rr.at[0], before).wait_send()
     remote(rimbuf, rim_a, rs.at[2], rr.at[2], follow).wait_send()
     pl.when(has_under)(lambda: remote(grimbuf, grim_b, rs.at[1], rr.at[1], under).wait_send())
@@ -427,17 +464,16 @@
         in_specs=[there] * 12,
         out_specs=(there, there),
         scratch_shapes=[
-            pltpu.VMEM((SUB, POS + 2, ROWS, C), BF16),
-            pltpu.VMEM((SUB, POS + 8, ROWS, C), BF16),
-            pltpu.VMEM((SUB, POS + 8, ROWS, C), BF16),
-            pltpu.VMEM((SUB, POS + 2, ROWS, C), BF16),
-            pltpu.VMEM((POS, 16, C), BF16),
+            pltpu.VMEM((SUB, WIDE, ROWS, C), BF16),
+            pltpu.VMEM((POS + 8, ROWS, C), BF16),
+            pltpu.VMEM((SUB, WIDE, ROWS, C), BF16),
+            pltpu.VMEM((NEAR, ROWS, C), BF16),
+            pltpu.VMEM((NEAR, 16, C), BF16),
             rim, rim, rim, rim, rim, rim,
-            pltpu.VMEM((SUB, M, C), F32),
-            pltpu.VMEM((SUB, M, 1), F32),
-            pltpu.VMEM((SUB, M, HID), F32),
-            pltpu.VMEM((SUB, M, C), F32),
-            pltpu.VMEM((SUB, M, C), F32),
+            pltpu.VMEM((SUB, MN, C), F32),
+            pltpu.VMEM((SUB, MN, 1), F32),
+            pltpu.VMEM((SUB, MN, HID), F32),
+            pltpu.VMEM((MN, C), F32),
             pltpu.VMEM((SUB, M, C), BF16),
             pltpu.VMEM((SUB, POS, ROWS, C), BF16),
             pltpu.VMEM((POS, 16, C), BF16),
@@ -450,7 +486,7 @@
             pltpu.VMEM((HID, C), BF16), pltpu.VMEM((C, HID), BF16),
             dma((SUB, POS)), dma((SUB, POS)),
             dma((POS,)), dma((POS,)),
-            dma((4, SUB, 2)), dma((4, SUB, 2)),
+            dma((3, SUB, 2)), dma((3, SUB, 2)),
             dma((SUB, POS)), dma((SUB, POS)),
             dma((POS,)), dma((POS,)),
             dma((4,)), dma((4,)),

time: 102 us -> 97.8 us (0.959)
  the two profiles are of different devices: /device:TPU:57 before, /device:TPU:59 now
where the time goes in v3:
time: 97.8 us; the launch traced here: 97.6 us
  Pallas kernels  93.5 us (96%)
  local copies, waits for them, and re-layouts  3.44 us (4%)
    pallas_call x1, Pallas kernels, body(): pl.pallas_call(kernel, out_shape=(jax.ShapeDtypeStruct(pooled_cotangent.s...  93.5 us
    unnamed x2, local copies, waits for them, and re-layouts  3.44 us

profile of v3, /device:TPU:59, one launch (start us, length us, event | category | flops | bytes accessed | tf_op | source)
XLA Modules:
  0.0 97.6 jit_solution(2314039939867767407)
XLA Ops:
  0.6 93.5 %shard_map.131 = (bf16[4,32,512]{2,1,0:T(8,128)(2,1)}, bf16[4,128,512]{2,1,0:T(8,128)(2,1)}) custom-call(bf16[4,128,512]{2,1,0:T(8,128)(2,1)} %x_ref.1, f32[3,512]{1,0:T(4,128)} %taps1_hbm.1, f32[1,512]{1,0:T(1,128)} %bitcast.2, bf16[512,1024]{1,0:T(8,128)(2,1)} %up1_hbm.1, bf16[1024,512]{1,0:T(8,128)(2,1)} %down1_hbm.1, f32[3,512]{1,0:T(4,128)} %taps2_hbm.1, ...), custom_call_target="tpu_custom_call" | custom-call | flops 4300000256 | bytes 8000000 | tf_op jit(solution)/shard_map/pallas_call | solution.py:458
  94.1 1.6 %copy.16 = bf16[4,32,512]{2,1,0:T(8,128)(2,1)} copy(bf16[4,32,512]{2,1,0:T(8,128)(2,1)} %get-tuple-element.4) | data formatting | bytes 262144
  95.7 1.9 %copy.17 = bf16[4,128,512]{2,1,0:T(8,128)(2,1)} copy(bf16[4,128,512]{2,1,0:T(8,128)(2,1)} %get-tuple-element.5) | data formatting | bytes 1048576

commit v4 on v3

--- a/solution.py
+++ b/solution.py
@@ -221,7 +221,6 @@
     send_x(1)
     send_g()
     send_x(2)
-    send_x(3)
 
     for copy in parameter_copies:
         copy.wait()
@@ -409,6 +408,7 @@
 
     def pipeline(t, carry):
         pl.when(t < SUB)(lambda: stage_a(t))
+        pl.when(t == 0)(lambda: send_x(3))
         pl.when(t == 1)(take_g)
         pl.when(t == 2)(share_g)
         pl.when(t == SUB)(take_g_rims)

time: 97.8 us -> 98.6 us (level)
  the two profiles are of different devices: /device:TPU:59 before, /device:TPU:68 now
where the time goes in v4:
time: 98.6 us; the launch traced here: 98.4 us
  Pallas kernels  94.3 us (96%)
  local copies, waits for them, and re-layouts  3.44 us (3%)
    pallas_call x1, Pallas kernels, body(): pl.pallas_call(kernel, out_shape=(jax.ShapeDtypeStruct(pooled_cotangent.s...  94.3 us
    unnamed x2, local copies, waits for them, and re-layouts  3.44 us

profile of v4, /device:TPU:68, one launch (start us, length us, event | category | flops | bytes accessed | tf_op | source)
XLA Modules:
  0.0 98.4 jit_solution(10194471289243119452)
XLA Ops:
  0.6 94.3 %shard_map.131 = (bf16[4,32,512]{2,1,0:T(8,128)(2,1)}, bf16[4,128,512]{2,1,0:T(8,128)(2,1)}) custom-call(bf16[4,128,512]{2,1,0:T(8,128)(2,1)} %x_ref.1, f32[3,512]{1,0:T(4,128)} %taps1_hbm.1, f32[1,512]{1,0:T(1,128)} %bitcast.2, bf16[512,1024]{1,0:T(8,128)(2,1)} %up1_hbm.1, bf16[1024,512]{1,0:T(8,128)(2,1)} %down1_hbm.1, f32[3,512]{1,0:T(4,128)} %taps2_hbm.1, ...), custom_call_target="tpu_custom_call" | custom-call | flops 4300000256 | bytes 8000000 | tf_op jit(solution)/shard_map/pallas_call | solution.py:458
  95.0 1.6 %copy.16 = bf16[4,32,512]{2,1,0:T(8,128)(2,1)} copy(bf16[4,32,512]{2,1,0:T(8,128)(2,1)} %get-tuple-element.4) | data formatting | bytes 262144
  96.5 1.9 %copy.17 = bf16[4,128,512]{2,1,0:T(8,128)(2,1)} copy(bf16[4,128,512]{2,1,0:T(8,128)(2,1)} %get-tuple-element.5) | data formatting | bytes 1048576
